TPU v7x, 32 devices: a whole 2x2x4 slice. The times are simulated.
32 devices in a mesh: dp: 8 (over y, x, core), expert: 4 (over z).
Axes of the slice: x: 2, y: 2, z: 4, core: 2. Of those that a mesh axis runs over, the one named last changes fastest.
Arguments:
- tokens: bfloat16 [1024, 2048], P(('dp', 'expert')), may hold values from -6 to 6
- gates: bfloat16 [1024, 2], P(('dp', 'expert')), may hold values from 0.019897461 to 0.5
- routes: int32 [1024, 2], P(('dp', 'expert')), may hold values from 0 to 3, all different within a row; in each aligned block of 32 rows (0 to 31, 32 to 63, ...) at most 24 rows name the same one
- cotangent: bfloat16 [1024, 2048], P(('dp', 'expert')), may hold values from -6 to 6
- up_weight: bfloat16 [4, 2048, 768], P('expert'), may hold values from -0.125 to 0.125
- down_weight: bfloat16 [4, 768, 2048], P('expert'), may hold values from -0.21875 to 0.21875
Outputs:
- mixed: bfloat16 [1024, 2048], P(('dp', 'expert'))
- grad_tokens: bfloat16 [1024, 2048], P(('dp', 'expert'))
- grad_down: float32 [4, 384, 1024], P('expert', 'dp')
Inputs may be any that keep to these rules, and one draw needn't show every extreme that they name: `routes`: each token names 2 different experts; among the tokens of one device no expert is named by more than 24 tokens, and in every draw some device's tokens name some expert exactly 24 times.
All inputs are finite; a program needn't handle non-finite values.
Results may differ from a plain program's by a relative error of at most 0.0066.
Values may be sent and summed in bfloat16 or wider, within the bound.
A program may use at most 64 MiB of HBM per device.

v0:
```python
import jax
import jax.numpy as jnp
from jax import lax
from jax.sharding import PartitionSpec as P


def slot_tables(route_blocks, gate_blocks, owners, capacity):
    matches = route_blocks == owners[:, None, None]
    chosen = jnp.sum(matches.astype(jnp.int32), axis=2)
    weights = jnp.sum(jnp.where(matches, gate_blocks.astype(jnp.float32), jnp.float32(0.0)), axis=2)
    ranks = jnp.cumsum(chosen, axis=1) - 1
    positions = jnp.arange(capacity, dtype=jnp.int32)
    placed = (chosen[:, None, :] == 1) & (ranks[:, None, :] == positions[None, :, None])
    placing = placed.astype(jnp.bfloat16)
    slot_gates = jnp.einsum(
        "bct,bt->bc", placing, weights.astype(jnp.bfloat16), preferred_element_type=jnp.float32
    )
    return (placing, slot_gates)


def expert_forward(rows, slot_gates, w_up, w_down):
    pre = jnp.einsum("scd,df->scf", rows, w_up, preferred_element_type=jnp.float32)
    hidden = jax.nn.silu(pre).astype(jnp.bfloat16)
    outputs = jnp.einsum("scf,fd->scd", hidden, w_down, preferred_element_type=jnp.float32)
    contrib = (slot_gates[..., None] * outputs).astype(jnp.bfloat16)
    return (contrib, pre, hidden)


def expert_backward(scaled, pre, w_up, w_down):
    d_hidden = jnp.einsum("scd,fd->scf", scaled, w_down, preferred_element_type=jnp.float32)
    sig = jax.nn.sigmoid(pre)
    d_pre = (d_hidden * sig * (1.0 + pre * (1.0 - sig))).astype(jnp.bfloat16)
    return jnp.einsum("scf,df->scd", d_pre, w_up, preferred_element_type=jnp.float32).astype(
        jnp.bfloat16
    )


def shards(tokens, gates, routes, cotangent, up_weight, down_weight):
    w_up = up_weight[0]
    w_down = down_weight[0]
    tok_dev, width = tokens.shape
    top = routes.shape[1]
    ff_width = w_up.shape[1]
    senders = lax.axis_size("expert")
    experts = senders * up_weight.shape[0]
    capacity = max(2, min(tok_dev, 3 * tok_dev * top // (2 * experts)))
    owners = jnp.arange(senders, dtype=jnp.int32)
    route_blocks = jnp.broadcast_to(routes[None], (senders, tok_dev, top))
    gate_blocks = jnp.broadcast_to(gates[None], (senders, tok_dev, top))
    placing, slot_gates = slot_tables(route_blocks, gate_blocks, owners, capacity)
    rows = jnp.einsum("sct,td->scd", placing, tokens, preferred_element_type=jnp.float32).astype(
        jnp.bfloat16
    )
    arrived = lax.all_to_all(rows, "expert", split_axis=0, concat_axis=0, tiled=True)
    arrived_gates = lax.all_to_all(
        slot_gates.astype(jnp.bfloat16), "expert", split_axis=0, concat_axis=0, tiled=True
    )
    contrib, pre_part, hidden_part = expert_forward(
        arrived, arrived_gates.astype(jnp.float32), w_up, w_down
    )
    returned_part = lax.all_to_all(contrib, "expert", split_axis=0, concat_axis=0, tiled=True)
    mixed = jnp.einsum(
        "sct,scd->td", placing, returned_part, preferred_element_type=jnp.float32
    ).astype(jnp.bfloat16)
    slot_cot = jnp.einsum(
        "sct,td->scd", placing, cotangent, preferred_element_type=jnp.float32
    ).astype(jnp.bfloat16)
    outgoing = (slot_gates[..., None] * slot_cot.astype(jnp.float32)).astype(jnp.bfloat16)
    scaled = lax.all_to_all(outgoing, "expert", split_axis=0, concat_axis=0, tiled=True)
    d_rows = expert_backward(scaled, pre_part, w_up, w_down)
    came_back = lax.all_to_all(d_rows, "expert", split_axis=0, concat_axis=0, tiled=True)
    grad_tokens = jnp.einsum(
        "sct,scd->td", placing, came_back, preferred_element_type=jnp.float32
    ).astype(jnp.bfloat16)
    window_ff = ff_width // 2
    window_d = width // 2
    flat_hidden = hidden_part.reshape(-1, ff_width)[:, :window_ff]
    flat_scaled = scaled.reshape(-1, width)[:, :window_d]
    grad_down = lax.psum_scatter(
        lax.dot_general(
            flat_hidden, flat_scaled, (((0,), (0,)), ((), ())), preferred_element_type=jnp.float32
        ),
        "dp",
        scatter_dimension=0,
        tiled=True,
    )
    return (mixed, grad_tokens, grad_down[None])


def solution(mesh):
    return jax.shard_map(
        shards,
        mesh=mesh,
        in_specs=(
            P(("dp", "expert"), None),
            P(("dp", "expert"), None),
            P(("dp", "expert"), None),
            P(("dp", "expert"), None),
            P("expert", None, None),
            P("expert", None, None),
        ),
        out_specs=(P(("dp", "expert"), None), P(("dp", "expert"), None), P("expert", "dp", None)),
        check_vma=False,
    )
```

profile of v0, /device:TPU:0, one launch (start us, length us, event | category | flops | bytes accessed | tf_op | source)
XLA Modules:
  0.0 91.1 jit_solution(17322372511627165408)
XLA Ops:
  7.2 0.0 copy-start
  7.2 0.8 convert_reduce_fusion
  8.0 0.2 reduce_window_sum.11
  8.2 1.9 %convolution_convert_fusion.1 = bf16[4,24,2048]{2,1,0:T(8,128)(2,1)} fusion(bf16[32,2048]{1,0:T(8,128)(2,1)} %param.6, s32[4,32]{1,0:T(4,128)S(1)} %broadcast_add_fusion, pred[4,32]{1,0:T(4,128)(4,1)S(1)} %broadcast_compare_fusion), kind=kOutput, calls=%fused_computation.14 | convolution fusion | flops 12785664 | bytes 524928 | tf_op jit(solution)/shard_map/sct,td->scd/dot_general | solution.py:51
  10.1 6.3 %all-to-all-start.1 = ((bf16[4,24,2048]{2,1,0:T(8,128)(2,1)}), bf16[4,24,2048]{2,1,0:T(8,128)(2,1)S(1)}, u32[]{:S(2)}, u32[]{:S(2)}) async-start(bf16[4,24,2048]{2,1,0:T(8,128)(2,1)} %convolution_convert_fusion.1), calls=%async_computation.1 | async-start | bytes 786432 | tf_op jit(solution)/shard_map/all_to_all | solution.py:54
  16.5 0.7 convert_element_type.55
  17.1 0.7 select_reduce_fusion
  17.8 0.1 fusion.47
  17.9 1.9 %fusion.16 = bf16[4,24,2048]{2,1,0:T(8,128)(2,1)} fusion(f32[4,24]{1,0:T(4,128)S(1)} %bitcast.59, bf16[32,2048]{1,0:T(8,128)(2,1)} %param.9, s32[4,32]{1,0:T(4,128)S(1)} %broadcast_add_fusion, pred[4,32]{1,0:T(4,128)(4,1)S(1)} %broadcast_compare_fusion), kind=kOutput, calls=%fused_computation.13 | convolution fusion | flops 13375488 | bytes 525312 | tf_op jit(solution)/shard_map/sct,td->scd/dot_general | solution.py:65
  19.8 8.3 %all-to-all-done.1 = bf16[4,24,2048]{2,1,0:T(8,128)(2,1)S(1)} async-done(((bf16[4,24,2048]{2,1,0:T(8,128)(2,1)}), bf16[4,24,2048]{2,1,0:T(8,128)(2,1)S(1)}, u32[]{:S(2)}, u32[]{:S(2)}) %all-to-all-start.1) | async-done | bytes 393248 | tf_op jit(solution)/shard_map/all_to_all | solution.py:54
  28.1 4.1 %all-to-all-start.3 = ((bf16[4,24,2048]{2,1,0:T(8,128)(2,1)}), bf16[4,24,2048]{2,1,0:T(8,128)(2,1)}, u32[]{:S(2)}, u32[]{:S(2)}) async-start(bf16[4,24,2048]{2,1,0:T(8,128)(2,1)} %fusion.16), calls=%async_computation.3 | async-start | bytes 786432 | tf_op jit(solution)/shard_map/all_to_all | solution.py:69
  32.3 0.0 reduce-scatter.2.cloned.1.call-start
  32.3 3.3 %multiply_convert_fusion = (bf16[4,24,768]{2,1,0:T(8,128)(2,1)}, f32[4,24,768]{2,1,0:T(8,128)}) fusion(bf16[4,24,2048]{2,1,0:T(8,128)(2,1)S(1)} %all-to-all-done.1, bf16[1,2048,768]{2,1,0:T(8,128)(2,1)} %param.10), kind=kOutput, calls=%fused_computation.26 | convolution fusion | flops 302358528 | bytes 3981312 | tf_op jit(solution)/shard_map/scd,df->scf/dot_general | solution.py:22
  35.6 0.0 copy-start.1
  35.6 7.6 %all-to-all-done.3 = bf16[4,24,2048]{2,1,0:T(8,128)(2,1)} async-done(((bf16[4,24,2048]{2,1,0:T(8,128)(2,1)}), bf16[4,24,2048]{2,1,0:T(8,128)(2,1)}, u32[]{:S(2)}, u32[]{:S(2)}) %all-to-all-start.3) | async-done | bytes 393248 | tf_op jit(solution)/shard_map/all_to_all | solution.py:69
  43.2 2.5 %fusion.36 = f32[384,1024]{1,0:T(8,128)} fusion(bf16[96,2048]{1,0:T(8,128)(2,1)} %bitcast.14, bf16[96,768]{1,0:T(8,128)(2,1)} %bitcast.58), kind=kOutput, calls=%fused_computation.28 | convolution fusion | flops 75497472 | bytes 1843200 | tf_op jit(solution)/shard_map/dot_general | solution.py:80
  45.7 0.0 reduce-scatter.2.cloned.1.call-update
  45.8 0.6 copy.14
  46.3 3.2 %all-to-all-start = ((bf16[4,1,24]{2,1,0:T(2,128)(2,1)}), bf16[4,1,24]{2,1,0:T(2,128)(2,1)S(1)}, u32[]{:S(2)}, u32[]{:S(2)}) async-start(bf16[4,1,24]{2,1,0:T(2,128)(2,1)} %copy.14), calls=%async_computation | async-start | bytes 4096 | tf_op jit(solution)/shard_map/all_to_all | solution.py:55
  49.6 0.0 copy-done
  49.6 0.0 copy-done.1
  49.6 5.2 %fusion.17 = bf16[4,24,2048]{2,1,0:T(8,128)(2,1)} fusion(bf16[1,2048,768]{2,1,0:T(8,128)(2,1)} %param.10, bf16[4,24,2048]{2,1,0:T(8,128)(2,1)} %all-to-all-done.3, bf16[1,768,2048]{2,1,0:T(8,128)(2,1)S(1)} %copy-done, f32[4,24,768]{2,1,0:T(8,128)S(1)} %copy-done.1), kind=kOutput, calls=%fused_computation.15 | convolution fusion | flops 604839936 | bytes 7372800 | tf_op jit(solution)/shard_map/scf,df->scd/dot_general | solution.py:33
  54.8 0.3 all-to-all-done
  55.0 4.8 %all-to-all-start.4 = ((bf16[4,24,2048]{2,1,0:T(8,128)(2,1)}), bf16[4,24,2048]{2,1,0:T(8,128)(2,1)S(1)}, u32[]{:S(2)}, u32[]{:S(2)}) async-start(bf16[4,24,2048]{2,1,0:T(8,128)(2,1)} %fusion.17), calls=%async_computation.4 | async-start | bytes 786432 | tf_op jit(solution)/shard_map/all_to_all | solution.py:71
  59.8 2.3 %fusion.11 = bf16[4,24,2048]{2,1,0:T(8,128)(2,1)} fusion(bf16[4,24,768]{2,1,0:T(8,128)(2,1)} %get-tuple-element.3, bf16[1,768,2048]{2,1,0:T(8,128)(2,1)S(1)} %copy-done, f32[4,24]{1,0:T(4,128)S(1)} %bitcast.61), kind=kOutput, calls=%fused_computation.9 | convolution fusion | flops 302383104 | bytes 3686784 | tf_op jit(solution)/shard_map/scf,fd->scd/dot_general | solution.py:24
  62.1 7.2 %all-to-all-done.4 = bf16[4,24,2048]{2,1,0:T(8,128)(2,1)S(1)} async-done(((bf16[4,24,2048]{2,1,0:T(8,128)(2,1)}), bf16[4,24,2048]{2,1,0:T(8,128)(2,1)S(1)}, u32[]{:S(2)}, u32[]{:S(2)}) %all-to-all-start.4) | async-done | bytes 393248 | tf_op jit(solution)/shard_map/all_to_all | solution.py:71
  69.3 4.1 %all-to-all-start.2 = ((bf16[4,24,2048]{2,1,0:T(8,128)(2,1)}), bf16[4,24,2048]{2,1,0:T(8,128)(2,1)}, u32[]{:S(2)}, u32[]{:S(2)}) async-start(bf16[4,24,2048]{2,1,0:T(8,128)(2,1)} %fusion.11), calls=%async_computation.2 | async-start | bytes 786432 | tf_op jit(solution)/shard_map/all_to_all | solution.py:61
  73.4 0.9 fusion.21
  74.3 8.0 %all-to-all-done.2 = bf16[4,24,2048]{2,1,0:T(8,128)(2,1)} async-done(((bf16[4,24,2048]{2,1,0:T(8,128)(2,1)}), bf16[4,24,2048]{2,1,0:T(8,128)(2,1)}, u32[]{:S(2)}, u32[]{:S(2)}) %all-to-all-start.2) | async-done | bytes 393248 | tf_op jit(solution)/shard_map/all_to_all | solution.py:61
  82.3 1.9 %fusion.20 = bf16[32,2048]{1,0:T(8,128)(2,1)} fusion(bf16[4,24,2048]{2,1,0:T(8,128)(2,1)} %all-to-all-done.2, s32[4,32]{1,0:T(4,128)S(1)} %broadcast_add_fusion, pred[4,32]{1,0:T(4,128)(4,1)S(1)} %broadcast_compare_fusion), kind=kOutput, calls=%fused_computation.18 | convolution fusion | flops 12654592 | bytes 524928 | tf_op jit(solution)/shard_map/sct,scd->td/dot_general | solution.py:62
  84.2 0.0 reduce-scatter.2.cloned.1.call-done
  (4 shorter events, 0.0 us)
Async XLA Ops:
  7.2 42.4 %copy-start = (bf16[1,768,2048]{2,1,0:T(8,128)(2,1)S(1)}, bf16[1,768,2048]{2,1,0:T(8,128)(2,1)}, u32[]{:S(2)}) copy-start(bf16[1,768,2048]{2,1,0:T(8,128)(2,1)} %param.11) | copy-start | bytes 9437188
  10.1 18.0 %all-to-all-start.1 = ((bf16[4,24,2048]{2,1,0:T(8,128)(2,1)}), bf16[4,24,2048]{2,1,0:T(8,128)(2,1)S(1)}, u32[]{:S(2)}, u32[]{:S(2)}) async-start(bf16[4,24,2048]{2,1,0:T(8,128)(2,1)} %convolution_convert_fusion.1), calls=%async_computation.1 | async-start | bytes 786432 | tf_op jit(solution)/shard_map/all_to_all | solution.py:54
  28.1 15.1 %all-to-all-start.3 = ((bf16[4,24,2048]{2,1,0:T(8,128)(2,1)}), bf16[4,24,2048]{2,1,0:T(8,128)(2,1)}, u32[]{:S(2)}, u32[]{:S(2)}) async-start(bf16[4,24,2048]{2,1,0:T(8,128)(2,1)} %fusion.16), calls=%async_computation.3 | async-start | bytes 786432 | tf_op jit(solution)/shard_map/all_to_all | solution.py:69
  32.3 52.0 %reduce-scatter.2.cloned.1.call-start = ((), (), s32[]{:S(2)}) async-start(), calls=%async_computation.6 | async-start | bytes 1769472 | tf_op jit(solution)/shard_map/reduce_scatter | solution.py:79
  35.6 14.0 %copy-start.1 = (f32[4,24,768]{2,1,0:T(8,128)S(1)}, f32[4,24,768]{2,1,0:T(8,128)}, u32[]{:S(2)}) copy-start(f32[4,24,768]{2,1,0:T(8,128)} %get-tuple-element.4) | copy-start | bytes 884740
  46.3 8.7 %all-to-all-start = ((bf16[4,1,24]{2,1,0:T(2,128)(2,1)}), bf16[4,1,24]{2,1,0:T(2,128)(2,1)S(1)}, u32[]{:S(2)}, u32[]{:S(2)}) async-start(bf16[4,1,24]{2,1,0:T(2,128)(2,1)} %copy.14), calls=%async_computation | async-start | bytes 4096 | tf_op jit(solution)/shard_map/all_to_all | solution.py:55
  55.0 14.2 %all-to-all-start.4 = ((bf16[4,24,2048]{2,1,0:T(8,128)(2,1)}), bf16[4,24,2048]{2,1,0:T(8,128)(2,1)S(1)}, u32[]{:S(2)}, u32[]{:S(2)}) async-start(bf16[4,24,2048]{2,1,0:T(8,128)(2,1)} %fusion.17), calls=%async_computation.4 | async-start | bytes 786432 | tf_op jit(solution)/shard_map/all_to_all | solution.py:71
  69.3 13.1 %all-to-all-start.2 = ((bf16[4,24,2048]{2,1,0:T(8,128)(2,1)}), bf16[4,24,2048]{2,1,0:T(8,128)(2,1)}, u32[]{:S(2)}, u32[]{:S(2)}) async-start(bf16[4,24,2048]{2,1,0:T(8,128)(2,1)} %fusion.11), calls=%async_computation.2 | async-start | bytes 786432 | tf_op jit(solution)/shard_map/all_to_all | solution.py:61
Sparse Core Ops, SparseCore 0:
  45.9 37.5 reduce-scatter.1
where the time goes:
time: 91.7 us; the launch traced here: 91.1 us
  waiting for transfers between devices  31.4 us (34%)
  starting transfers between devices  22.6 us (25%)
  matrix products  20 us (22%)
  between operations  14.1 us (15%)
  other arithmetic  2.42 us (3%)
    all_to_all x1, waiting for transfers between devices, shards(): lax.all_to_all(rows, 'expert', split_axis=0, concat_axis=0, tiled=True)  8.3 us
    all_to_all x1, waiting for transfers between devices, shards(): lax.all_to_all(contrib, 'expert', split_axis=0, concat_axis=0, tiled=True)  8.04 us
    all_to_all x1, waiting for transfers between devices, shards(): lax.all_to_all(outgoing, 'expert', split_axis=0, concat_axis=0, tiled=True)  7.61 us
    all_to_all x1, waiting for transfers between devices, shards(): lax.all_to_all(d_rows, 'expert', split_axis=0, concat_axis=0, tiled=True)  7.16 us
    all_to_all x1, starting transfers between devices, shards(): lax.all_to_all(rows, 'expert', split_axis=0, concat_axis=0, tiled=True)  6.32 us
    dot_general x1, matrix products, expert_backward(): jnp.einsum('scf,df->scd', d_pre, w_up, preferred_element_type=jnp.float32)  5.16 us
    all_to_all x1, starting transfers between devices, shards(): lax.all_to_all(d_rows, 'expert', split_axis=0, concat_axis=0, tiled=True)  4.77 us
    all_to_all x1, starting transfers between devices, shards(): lax.all_to_all(contrib, 'expert', split_axis=0, concat_axis=0, tiled=True)  4.11 us
  transfers between devices with their start and end apart: 6, of which 5 were waited for; matrix products, arithmetic and copies ran while one was open for 19% of the time, Pallas kernels for 0%

commit v1 on v0

--- a/solution.py
+++ b/solution.py
@@ -1,7 +1,362 @@
+import functools
+
 import jax
 import jax.numpy as jnp
 from jax import lax
+from jax.experimental import pallas as pl
+from jax.experimental.pallas import tpu as pltpu
 from jax.sharding import PartitionSpec as P
+
+F32, BF16 = jnp.float32, jnp.bfloat16
+N = 4
+CH = 4
+MESH = pl.DeviceIdType.MESH
+
+
+def dot(a, b, ca, cb):
+    return lax.dot_general(a, b, (((ca,), (cb,)), ((), ())), preferred_element_type=F32)
+
+
+def layer_kernel(
+    tok, gates, routes, cot, wu, wd,
+    mixed, gtok, gdown,
+    X, G, SC, Y, R, WU, WD, WG, pre, dh, hid, dpre, GD, S1, R1, S2, R2,
+    loc, ag_s, ag_r, rs_s, rs_r, g_s, g_r, p1_s, p1_r, p2_s, p2_r,
+):
+    T = tok.shape[0]
+    W = X.shape[2]
+    sh = gdown.shape[0]
+    hw = GD.shape[0]
+    cols = [slice(c * W, (c + 1) * W) for c in range(CH)]
+    z = lax.axis_index("expert")
+    p = lax.axis_index("dp")
+    core, chip = lax.rem(p, 2), lax.div(p, 2)
+    cx, cy = lax.rem(chip, 2), lax.div(chip, 2)
+    mates = [chip, (1 - cx) + 2 * cy, cx + 2 * (1 - cy), (1 - cx) + 2 * (1 - cy)]
+    other = 2 * chip + 1 - core
+
+    def rows(s):
+        return pl.ds(s * T, T)
+
+    def here(fn):
+        for k in range(N):
+            pl.when(z == k)(functools.partial(fn, k))
+
+    own = pl.ds(pl.multiple_of(z * T, T), T)
+    locals_ = {}
+    for c in range(CH):
+        locals_["x", c] = pltpu.make_async_copy(tok.at[:, pl.ds(c * W, W)], X.at[c, own], loc.at[0, c])
+        locals_["g", c] = pltpu.make_async_copy(cot.at[:, pl.ds(c * W, W)], G.at[c, own], loc.at[1, c])
+        locals_["u", c] = pltpu.make_async_copy(wu.at[0, pl.ds(c * W, W)], WU.at[c], loc.at[2, c])
+        locals_["d", c] = pltpu.make_async_copy(wd.at[0, :, pl.ds(c * W, W)], WD.at[c], loc.at[3, c])
+    for name in "xgud":
+        for c in range(CH):
+            locals_[name, c].start()
+
+    barrier = pltpu.get_barrier_semaphore()
+    for d in range(1, N):
+        pl.semaphore_signal(barrier, inc=1, device_id={"expert": lax.rem(z + d, N)}, device_id_type=MESH)
+    for peer in [other] + [2 * m + core for m in mates[1:]]:
+        pl.semaphore_signal(barrier, inc=1, device_id={"dp": peer}, device_id_type=MESH)
+
+    lane = lax.broadcasted_iota(jnp.int32, (T, WG.shape[1]), 1)
+    table = jnp.zeros(lane.shape, F32)
+    for j in range(routes.shape[1]):
+        table += jnp.where(routes[:, j : j + 1] == lane, gates[:, j : j + 1].astype(F32), 0.0)
+    WG[own, :] = table.astype(BF16)
+    for c in range(CH):
+        locals_["x", c].wait()
+    pl.semaphore_wait(barrier, 7)
+
+    def ag(ph, c, s, k, step):
+        buf = (X, G)[ph].at[c, rows(s)]
+        return pltpu.make_async_remote_copy(
+            src_ref=buf, dst_ref=buf,
+            send_sem=ag_s.at[ph, c, s, (step + 1) // 2], recv_sem=ag_r.at[ph, c, s],
+            device_id={"expert": k + step}, device_id_type=MESH,
+        )
+
+    def ag_sends(ph, c, k, h):
+        if h == 0:
+            return [ag(ph, c, k, k, st) for st in (1, -1) if 0 <= k + st < N]
+        out = []
+        for st in (1, -1):
+            if 0 <= k - st * h < N and 0 <= k + st < N:
+                out.append(ag(ph, c, k - st * h, k, st))
+        return out
+
+    def ag_step(ph, c, h):
+        def fn(k):
+            for st in (1, -1):
+                s = k - st * h
+                if 0 <= s < N:
+                    ag(ph, c, s, k, st).wait_recv()
+                    if 0 <= k + st < N:
+                        ag(ph, c, s, k, st).start()
+
+        here(fn)
+
+    def ag_open(ph):
+        def fn(k):
+            for c in range(CH):
+                for cp in ag_sends(ph, c, k, 0):
+                    cp.start()
+
+        here(fn)
+
+    def rs(ph, c, s, k):
+        step = 1 if s > k else -1
+        slot = s + 1 if step == 1 else s
+        return pltpu.make_async_remote_copy(
+            src_ref=Y.at[ph, c, rows(s)], dst_ref=R.at[ph, c, rows(slot)],
+            send_sem=rs_s.at[ph, c, s], recv_sem=rs_r.at[ph, c, slot],
+            device_id={"expert": k + step}, device_id_type=MESH,
+        )
+
+    def rs_arrived(ph, c, s, k, step):
+        slot = s + 1 if step == 1 else s
+        pltpu.make_async_remote_copy(
+            src_ref=Y.at[ph, c, rows(s)], dst_ref=R.at[ph, c, rows(slot)],
+            send_sem=rs_s.at[ph, c, s], recv_sem=rs_r.at[ph, c, slot],
+            device_id={"expert": k - step}, device_id_type=MESH,
+        ).wait_recv()
+        return R[ph, c, rows(slot), :].astype(F32)
+
+    def rs_open(ph, c):
+        @pl.when(z == 0)
+        def _():
+            for s in range(N - 1, 0, -1):
+                rs(ph, c, s, 0).start()
+
+        @pl.when(z == N - 1)
+        def _():
+            for s in range(N - 1):
+                rs(ph, c, s, N - 1).start()
+
+    def rs_pass(ph, c):
+        def fn(k, step, targets):
+            for s in targets:
+                got = rs_arrived(ph, c, s, k, step)
+                Y[ph, c, rows(s), :] = (Y[ph, c, rows(s), :].astype(F32) + got).astype(BF16)
+                rs(ph, c, s, k).start()
+
+        for h in range(1, N - 1):
+            k = h
+            pl.when(z == k)(functools.partial(fn, k, 1, list(range(N - 1, k, -1))))
+            k = N - 1 - h
+            pl.when(z == k)(functools.partial(fn, k, -1, list(range(k))))
+
+    def rs_close(ph, c):
+        out = (mixed, gtok)[ph]
+
+        def fn(k):
+            total = Y[ph, c, rows(k), :].astype(F32)
+            if k > 0:
+                total += rs_arrived(ph, c, k, k, 1)
+            if k < N - 1:
+                total += rs_arrived(ph, c, k, k, -1)
+            out[:, cols[c]] = total.astype(BF16)
+
+        here(fn)
+
+    def gate(k, s):
+        return pltpu.make_async_remote_copy(
+            src_ref=WG.at[rows(k)], dst_ref=WG.at[rows(k)],
+            send_sem=g_s.at[s], recv_sem=g_r.at[k],
+            device_id={"expert": s}, device_id_type=MESH,
+        )
+
+    ag_open(0)
+
+    def gate_open(k):
+        for s in range(N):
+            if s != k:
+                gate(k, s).start()
+
+    here(gate_open)
+
+    def up(c):
+        locals_["u", c].wait()
+        part = dot(X[c], WU[c], 1, 0)
+        pre[...] = part if c == 0 else pre[...] + part
+
+    for t in range(CH + 2):
+        if t < CH:
+            ag_step(0, t, 1)
+        if 0 <= t - 1 < CH:
+            ag_step(0, t - 1, 2)
+        if t == CH:
+            for c in range(CH):
+                locals_["g", c].wait()
+            ag_open(1)
+        if 0 <= t - 2 < CH:
+            ag_step(0, t - 2, 3)
+            up(t - 2)
+
+    def gate_close(k):
+        for s in range(N):
+            if s != k:
+                gate(s, k).wait_recv()
+
+    here(gate_close)
+    wide = WG[...].astype(F32)
+    gcol = jnp.sum(
+        jnp.where(lax.broadcasted_iota(jnp.int32, wide.shape, 1) == z, wide, 0.0), axis=1, keepdims=True
+    )
+    v = pre[...]
+    hid[...] = (v / (1.0 + jnp.exp(-v))).astype(BF16)
+
+    def down(c):
+        locals_["d", c].wait()
+        Y[0, c] = (gcol * dot(hid[...], WD[c], 1, 0)).astype(BF16)
+
+    def back(c):
+        SC[c] = (gcol * G[c].astype(F32)).astype(BF16)
+        part = dot(SC[c], WD[c], 1, 1)
+        dh[...] = part if c == 0 else dh[...] + part
+
+    def plane1(m):
+        return pltpu.make_async_remote_copy(
+            src_ref=S1.at[m], dst_ref=R1.at[m], send_sem=p1_s.at[m], recv_sem=p1_r.at[m],
+            device_id={"dp": other}, device_id_type=MESH,
+        )
+
+    def plane2(d):
+        return pltpu.make_async_remote_copy(
+            src_ref=S2.at[d - 1], dst_ref=R2.at[d - 1], send_sem=p2_s.at[d - 1], recv_sem=p2_r.at[d - 1],
+            device_id={"dp": 2 * mates[d] + core}, device_id_type=MESH,
+        )
+
+    def shard(i):
+        return pl.ds(pl.multiple_of(i * sh, 16), sh)
+
+    def grads():
+        half = hid[:, :hw]
+        for c in range(CH // 2):
+            GD[:, cols[c]] = dot(half, SC[c], 0, 0)
+        for m in range(4):
+            S1[m] = GD[shard(2 * m + 1 - core), :].astype(BF16)
+            plane1(m).start()
+
+    for c in range(CH):
+        down(c)
+        rs_open(0, c)
+        ag_step(1, c, 1)
+        if c >= 1:
+            ag_step(1, c - 1, 2)
+            rs_pass(0, c - 1)
+    ag_step(1, CH - 1, 2)
+    rs_pass(0, CH - 1)
+    for c in range(CH):
+        ag_step(1, c, 3)
+        back(c)
+        if c == CH // 2 - 1:
+            grads()
+
+    sig = 1.0 / (1.0 + jnp.exp(-pre[...]))
+    dpre[...] = (dh[...] * sig * (1.0 + pre[...] * (1.0 - sig))).astype(BF16)
+
+    def drows(c):
+        Y[1, c] = dot(dpre[...], WU[c], 1, 1).astype(BF16)
+        rs_open(1, c)
+
+    for c in range(CH):
+        drows(c)
+        if c == 0:
+            for m in range(4):
+                plane1(m).wait_recv()
+            for d in range(1, 4):
+                S2[d - 1] = (
+                    GD[shard(2 * mates[d] + core), :] + R1[mates[d]].astype(F32)
+                ).astype(BF16)
+                plane2(d).start()
+        if c >= 1:
+            rs_pass(1, c - 1)
+    for c in range(CH):
+        rs_close(0, c)
+    rs_pass(1, CH - 1)
+    total = GD[shard(2 * chip + core), :] + R1[chip].astype(F32)
+    for d in range(1, 4):
+        plane2(d).wait_recv()
+        total += R2[d - 1].astype(F32)
+    gdown[...] = total
+    for c in range(CH):
+        rs_close(1, c)
+
+    def drain(k):
+        for ph in range(2):
+            for c in range(CH):
+                for h in range(N - 1):
+                    for cp in ag_sends(ph, c, k, h):
+                        cp.wait_send()
+                for s in range(N):
+                    if s != k:
+                        rs(ph, c, s, k).wait_send()
+        for s in range(N):
+            if s != k:
+                gate(k, s).wait_send()
+
+    here(drain)
+    for m in range(4):
+        plane1(m).wait_send()
+    for d in range(1, 4):
+        plane2(d).wait_send()
+
+
+def fused(tokens, gates, routes, cotangent, up_weight, down_weight):
+    T, D = tokens.shape
+    FF = up_weight.shape[2]
+    W = D // CH
+    hw, dw = FF // 2, D // 2
+    sh = hw // 8
+    A = N * T
+    dma = pltpu.SemaphoreType.DMA
+    anyspace = pl.BlockSpec(memory_space=pl.ANY)
+    vmem = pl.BlockSpec(memory_space=pltpu.VMEM)
+    mixed, gtok, gdown = pl.pallas_call(
+        layer_kernel,
+        out_shape=(
+            jax.ShapeDtypeStruct((T, D), BF16),
+            jax.ShapeDtypeStruct((T, D), BF16),
+            jax.ShapeDtypeStruct((sh, dw), F32),
+        ),
+        in_specs=[anyspace, vmem, vmem, anyspace, anyspace, anyspace],
+        out_specs=(vmem, vmem, vmem),
+        scratch_shapes=[
+            pltpu.VMEM((CH, A, W), BF16),
+            pltpu.VMEM((CH, A, W), BF16),
+            pltpu.VMEM((CH, A, W), BF16),
+            pltpu.VMEM((2, CH, A, W), BF16),
+            pltpu.VMEM((2, CH, A + T, W), BF16),
+            pltpu.VMEM((CH, W, FF), BF16),
+            pltpu.VMEM((CH, FF, W), BF16),
+            pltpu.VMEM((A, 128), BF16),
+            pltpu.VMEM((A, FF), F32),
+            pltpu.VMEM((A, FF), F32),
+            pltpu.VMEM((A, FF), BF16),
+            pltpu.VMEM((A, FF), BF16),
+            pltpu.VMEM((hw, dw), F32),
+            pltpu.VMEM((4, sh, dw), BF16),
+            pltpu.VMEM((4, sh, dw), BF16),
+            pltpu.VMEM((3, sh, dw), BF16),
+            pltpu.VMEM((3, sh, dw), BF16),
+            dma((4, CH)),
+            dma((2, CH, N, 2)),
+            dma((2, CH, N)),
+            dma((2, CH, N)),
+            dma((2, CH, N + 1)),
+            dma((N,)),
+            dma((N,)),
+            dma((4,)),
+            dma((4,)),
+            dma((3,)),
+            dma((3,)),
+        ],
+        compiler_params=pltpu.CompilerParams(
+            collective_id=0, has_side_effects=True, vmem_limit_bytes=44 * 1024 * 1024
+        ),
+    )(tokens, gates, routes, cotangent, up_weight, down_weight)
+    return (mixed, gtok, gdown[None])
 
 
 def slot_tables(route_blocks, gate_blocks, owners, capacity):
@@ -88,8 +443,9 @@
 
 
 def solution(mesh):
+    chain = mesh.shape["dp"] == 8 and mesh.shape["expert"] == N
     return jax.shard_map(
-        shards,
+        fused if chain else shards,
         mesh=mesh,
         in_specs=(
             P(("dp", "expert"), None),

time: 91.7 us -> 70.3 us (0.77)
  Pallas kernels: 0 us -> 60.3 us
  waiting for transfers between devices: 31.4 us -> 0 us
  starting transfers between devices: 22.6 us -> 0 us
  matrix products: 20 us -> 0 us
  between operations: 14.1 us -> 0.64 us
  local copies, waits for them, and re-layouts: 0.59 us -> 9.09 us
  other arithmetic: 2.42 us -> 0 us
    pallas_call x0 -> x1, Pallas kernels: none -> 60.3 us  [fused(): pl.pallas_call(layer_kernel, out_shape=(jax.ShapeDtypeStruct((T, D), BF16...]
    all_to_all x5 -> x0, waiting for transfers between devices: 31.4 us -> none  [the longest x1 8.3 us: shards(): lax.all_to_all(rows, 'expert', split_axis=0, concat_axis=0, tiled=True)]
    all_to_all x5 -> x0, starting transfers between devices: 22.5 us -> none  [the longest x1 6.32 us: shards(): lax.all_to_all(rows, 'expert', split_axis=0, concat_axis=0, tiled=True)]
    dot_general x9 -> x0, matrix products: 20 us -> none  [the longest x1 5.16 us: expert_backward(): jnp.einsum('scf,df->scd', d_pre, w_up, preferred_element_type=jnp.float32)]
    unnamed x4 -> x13, local copies, waits for them, and re-layouts: 0.01 us -> 9.09 us
    reduce_sum x2 -> x0, other arithmetic: 1.54 us -> none  [the longest x1 0.84 us: slot_tables(): chosen = jnp.sum(matches.astype(jnp.int32), axis=2)]
  transfers between devices with their start and end apart: 6 -> 0, of which waited for: 5 -> 0; matrix products, arithmetic and copies ran while one was open for 19% -> 0% of each run, Pallas kernels for 0% -> 0%
where the time goes in v1:
time: 70.3 us; the launch traced here: 70 us
  Pallas kernels  60.3 us (86%)
  local copies, waits for them, and re-layouts  9.09 us (13%)
    pallas_call x1, Pallas kernels, fused(): pl.pallas_call(layer_kernel, out_shape=(jax.ShapeDtypeStruct((T, D), BF16...  60.3 us
    unnamed x13, local copies, waits for them, and re-layouts  9.09 us

profile of v1, /device:TPU:0, one launch (start us, length us, event | category | flops | bytes accessed | tf_op | source)
XLA Modules:
  0.0 70.0 jit_solution(7441906928509463908)
XLA Ops:
  0.6 0.8 %copy.9.gates = bf16[32,2]{1,0:T(8,128)(2,1)S(1)} copy(bf16[32,2]{0,1:T(2,128)(2,1)} %param.7) | data formatting | bytes 256 | tf_op args[1]
  1.4 0.8 %copy.10.routes = s32[32,2]{1,0:T(8,128)S(1)} copy(s32[32,2]{0,1:T(2,128)} %param.8) | data formatting | bytes 512 | tf_op args[2]
  2.1 0.0 copy-start
  2.1 1.9 %copy-done = bf16[1,2048,768]{2,1,0:T(8,128)(2,1)S(1)} copy-done((bf16[1,2048,768]{2,1,0:T(8,128)(2,1)S(1)}, bf16[1,2048,768]{2,1,0:T(8,128)(2,1)}, u32[]{:S(2)}) %copy-start) | copy-done | bytes 3145752
  4.0 0.0 copy-start.1
  4.0 1.9 %copy-done.1 = bf16[1,768,2048]{2,1,0:T(8,128)(2,1)S(1)} copy-done((bf16[1,768,2048]{2,1,0:T(8,128)(2,1)S(1)}, bf16[1,768,2048]{2,1,0:T(8,128)(2,1)}, u32[]{:S(2)}) %copy-start.1) | copy-done | bytes 3145752
  5.9 0.0 copy-start.2
  5.9 0.9 %copy-done.2 = bf16[32,2048]{1,0:T(8,128)(2,1)S(1)} copy-done((bf16[32,2048]{1,0:T(8,128)(2,1)S(1)}, bf16[32,2048]{1,0:T(8,128)(2,1)}, u32[]{:S(2)}) %copy-start.2) | copy-done | bytes 131096
  6.8 0.0 copy-start.3
  6.8 0.9 %copy-done.3 = bf16[32,2048]{1,0:T(8,128)(2,1)S(1)} copy-done((bf16[32,2048]{1,0:T(8,128)(2,1)S(1)}, bf16[32,2048]{1,0:T(8,128)(2,1)}, u32[]{:S(2)}) %copy-start.3) | copy-done | bytes 131096
  7.7 60.3 %shard_map.85 = (bf16[32,2048]{1,0:T(8,128)(2,1)S(1)}, bf16[32,2048]{1,0:T(8,128)(2,1)S(1)}, f32[48,1024]{1,0:T(8,128)S(1)}) custom-call(bf16[32,2048]{1,0:T(8,128)(2,1)S(1)} %copy-done.2, bf16[32,2]{1,0:T(8,128)(2,1)S(1)} %copy.9.gates, s32[32,2]{1,0:T(8,128)S(1)} %copy.10.routes, bf16[32,2048]{1,0:T(8,128)(2,1)S(1)} %copy-done.3, ...), custom_call_target="tpu_custom_call" | custom-call | tf_op jit(solution)/shard_map/pallas_call | solution.py:316
  68.0 0.7 copy.14
  68.7 0.7 copy.15
  69.4 0.7 copy.16
Async XLA Ops:
  2.1 1.9 %copy-start = (bf16[1,2048,768]{2,1,0:T(8,128)(2,1)S(1)}, bf16[1,2048,768]{2,1,0:T(8,128)(2,1)}, u32[]{:S(2)}) copy-start(bf16[1,2048,768]{2,1,0:T(8,128)(2,1)} %wu.1) | copy-start | bytes 9437188
  4.0 1.9 %copy-start.1 = (bf16[1,768,2048]{2,1,0:T(8,128)(2,1)S(1)}, bf16[1,768,2048]{2,1,0:T(8,128)(2,1)}, u32[]{:S(2)}) copy-start(bf16[1,768,2048]{2,1,0:T(8,128)(2,1)} %wd.1) | copy-start | bytes 9437188
  5.9 0.9 %copy-start.2 = (bf16[32,2048]{1,0:T(8,128)(2,1)S(1)}, bf16[32,2048]{1,0:T(8,128)(2,1)}, u32[]{:S(2)}) copy-start(bf16[32,2048]{1,0:T(8,128)(2,1)} %tok.1) | copy-start | bytes 393220
  6.8 0.9 %copy-start.3 = (bf16[32,2048]{1,0:T(8,128)(2,1)S(1)}, bf16[32,2048]{1,0:T(8,128)(2,1)}, u32[]{:S(2)}) copy-start(bf16[32,2048]{1,0:T(8,128)(2,1)} %cot.1) | copy-start | bytes 393220

commit v2 on v1

--- a/solution.py
+++ b/solution.py
@@ -10,6 +10,7 @@
 F32, BF16 = jnp.float32, jnp.bfloat16
 N = 4
 CH = 4
+WINDOW = 4
 MESH = pl.DeviceIdType.MESH
 
 
@@ -59,11 +60,12 @@
     for peer in [other] + [2 * m + core for m in mates[1:]]:
         pl.semaphore_signal(barrier, inc=1, device_id={"dp": peer}, device_id_type=MESH)
 
-    lane = lax.broadcasted_iota(jnp.int32, (T, WG.shape[1]), 1)
-    table = jnp.zeros(lane.shape, F32)
-    for j in range(routes.shape[1]):
-        table += jnp.where(routes[:, j : j + 1] == lane, gates[:, j : j + 1].astype(F32), 0.0)
-    WG[own, :] = table.astype(BF16)
+    expert = lax.broadcasted_iota(jnp.int32, (WG.shape[1], T), 0)
+    table = jnp.zeros(expert.shape, F32)
+    for j in range(routes.shape[0]):
+        table += jnp.where(routes[j : j + 1, :] == expert, gates[j : j + 1, :].astype(F32), 0.0)
+    eye = lax.broadcasted_iota(jnp.int32, (T, T), 0) == lax.broadcasted_iota(jnp.int32, (T, T), 1)
+    WG[own, :] = dot(eye.astype(F32).astype(BF16), table.astype(BF16), 1, 1).astype(BF16)
     for c in range(CH):
         locals_["x", c].wait()
     pl.semaphore_wait(barrier, 7)
@@ -122,29 +124,37 @@
         ).wait_recv()
         return R[ph, c, rows(slot), :].astype(F32)
 
-    def rs_open(ph, c):
-        @pl.when(z == 0)
-        def _():
-            for s in range(N - 1, 0, -1):
-                rs(ph, c, s, 0).start()
-
-        @pl.when(z == N - 1)
-        def _():
-            for s in range(N - 1):
-                rs(ph, c, s, N - 1).start()
-
-    def rs_pass(ph, c):
-        def fn(k, step, targets):
-            for s in targets:
-                got = rs_arrived(ph, c, s, k, step)
-                Y[ph, c, rows(s), :] = (Y[ph, c, rows(s), :].astype(F32) + got).astype(BF16)
-                rs(ph, c, s, k).start()
-
-        for h in range(1, N - 1):
-            k = h
-            pl.when(z == k)(functools.partial(fn, k, 1, list(range(N - 1, k, -1))))
-            k = N - 1 - h
-            pl.when(z == k)(functools.partial(fn, k, -1, list(range(k))))
+    def rs_open(ph):
+        def fn(k, targets):
+            sent = [rs(ph, c, s, k) for s in targets for c in range(CH)]
+            for i, cp in enumerate(sent):
+                if i >= WINDOW:
+                    sent[i - WINDOW].wait_send()
+                cp.start()
+
+        pl.when(z == 0)(functools.partial(fn, 0, list(range(N - 1, 0, -1))))
+        pl.when(z == N - 1)(functools.partial(fn, N - 1, list(range(N - 1))))
+
+    def rs_left(k):
+        targets = list(range(N - 1, 0, -1)) if k == 0 else [s for s in range(N) if s != k]
+        every = [(s, c) for s in targets for c in range(CH)]
+        return every[-WINDOW:] if k in (0, N - 1) else every
+
+    def rs_pass(ph):
+        def add(c, s, k, step):
+            got = rs_arrived(ph, c, s, k, step)
+            Y[ph, c, rows(s), :] = (Y[ph, c, rows(s), :].astype(F32) + got).astype(BF16)
+            rs(ph, c, s, k).start()
+
+        def fn(k, step, far, near, back_to):
+            for c in range(CH):
+                add(c, far, k, step)
+            for c in range(CH):
+                add(c, near, k, step)
+                add(c, back_to, k, -step)
+
+        pl.when(z == 1)(functools.partial(fn, 1, 1, 3, 2, 0))
+        pl.when(z == 2)(functools.partial(fn, 2, -1, 0, 1, 3))
 
     def rs_close(ph, c):
         out = (mixed, gtok)[ph]
@@ -240,13 +250,11 @@
 
     for c in range(CH):
         down(c)
-        rs_open(0, c)
+    rs_open(0)
+    for c in range(CH):
         ag_step(1, c, 1)
-        if c >= 1:
-            ag_step(1, c - 1, 2)
-            rs_pass(0, c - 1)
-    ag_step(1, CH - 1, 2)
-    rs_pass(0, CH - 1)
+    for c in range(CH):
+        ag_step(1, c, 2)
     for c in range(CH):
         ag_step(1, c, 3)
         back(c)
@@ -255,26 +263,18 @@
 
     sig = 1.0 / (1.0 + jnp.exp(-pre[...]))
     dpre[...] = (dh[...] * sig * (1.0 + pre[...] * (1.0 - sig))).astype(BF16)
-
-    def drows(c):
+    for c in range(CH):
         Y[1, c] = dot(dpre[...], WU[c], 1, 1).astype(BF16)
-        rs_open(1, c)
-
-    for c in range(CH):
-        drows(c)
-        if c == 0:
-            for m in range(4):
-                plane1(m).wait_recv()
-            for d in range(1, 4):
-                S2[d - 1] = (
-                    GD[shard(2 * mates[d] + core), :] + R1[mates[d]].astype(F32)
-                ).astype(BF16)
-                plane2(d).start()
-        if c >= 1:
-            rs_pass(1, c - 1)
+    for m in range(4):
+        plane1(m).wait_recv()
+    for d in range(1, 4):
+        S2[d - 1] = (GD[shard(2 * mates[d] + core), :] + R1[mates[d]].astype(F32)).astype(BF16)
+        plane2(d).start()
+    rs_open(1)
+    rs_pass(0)
+    rs_pass(1)
     for c in range(CH):
         rs_close(0, c)
-    rs_pass(1, CH - 1)
     total = GD[shard(2 * chip + core), :] + R1[chip].astype(F32)
     for d in range(1, 4):
         plane2(d).wait_recv()
@@ -289,9 +289,8 @@
                 for h in range(N - 1):
                     for cp in ag_sends(ph, c, k, h):
                         cp.wait_send()
-                for s in range(N):
-                    if s != k:
-                        rs(ph, c, s, k).wait_send()
+            for s, c in rs_left(k):
+                rs(ph, c, s, k).wait_send()
         for s in range(N):
             if s != k:
                 gate(k, s).wait_send()
@@ -353,9 +352,9 @@
             dma((3,)),
         ],
         compiler_params=pltpu.CompilerParams(
-            collective_id=0, has_side_effects=True, vmem_limit_bytes=44 * 1024 * 1024
+            collective_id=0, has_side_effects=True, vmem_limit_bytes=60 * 1024 * 1024
         ),
-    )(tokens, gates, routes, cotangent, up_weight, down_weight)
+    )(tokens, gates.T, routes.T, cotangent, up_weight, down_weight)
     return (mixed, gtok, gdown[None])
 
 

time: 70.3 us -> 51.5 us (0.73)
  Pallas kernels: 60.3 us -> 45.9 us
  local copies, waits for them, and re-layouts: 9.09 us -> 4.75 us
    pallas_call x1, Pallas kernels: 60.3 us -> 45.9 us  [fused(): pl.pallas_call(layer_kernel, out_shape=(jax.ShapeDtypeStruct((T, D), BF16...]
    unnamed x13 -> x3, local copies, waits for them, and re-layouts: 9.09 us -> 4.75 us
where the time goes in v2:
time: 51.5 us; the launch traced here: 51.3 us
  Pallas kernels  45.9 us (89%)
  local copies, waits for them, and re-layouts  4.75 us (9%)
  between operations  0.64 us (1%)
    pallas_call x1, Pallas kernels, fused(): pl.pallas_call(layer_kernel, out_shape=(jax.ShapeDtypeStruct((T, D), BF16...  45.9 us
    unnamed x3, local copies, waits for them, and re-layouts  4.75 us

profile of v2, /device:TPU:0, one launch (start us, length us, event | category | flops | bytes accessed | tf_op | source)
XLA Modules:
  0.0 51.3 jit_solution(10444736535563958926)
XLA Ops:
  0.6 45.9 %shard_map.85 = (bf16[32,2048]{1,0:T(8,128)(2,1)}, bf16[32,2048]{1,0:T(8,128)(2,1)}, f32[48,1024]{1,0:T(8,128)}) custom-call(bf16[32,2048]{1,0:T(8,128)(2,1)} %tok.1, bf16[2,32]{1,0:T(2,128)(2,1)} %bitcast.5, s32[2,32]{1,0:T(2,128)} %bitcast.4, bf16[32,2048]{1,0:T(8,128)(2,1)} %cot.1, bf16[1,2048,768]{2,1,0:T(8,128)(2,1)} %wu.1, bf16[1,768,2048]{2,1,0:T(8,128)(2,1)} %wd.1), custom_call_target="tpu_custom_call" | custom-call | tf_op jit(solution)/shard_map/pallas_call | solution.py:315
  46.5 1.6 %copy.12 = bf16[32,2048]{1,0:T(8,128)(2,1)} copy(bf16[32,2048]{1,0:T(8,128)(2,1)} %get-tuple-element.12) | data formatting | bytes 262144
  48.1 1.6 %copy.13 = bf16[32,2048]{1,0:T(8,128)(2,1)} copy(bf16[32,2048]{1,0:T(8,128)(2,1)} %get-tuple-element.13) | data formatting | bytes 262144
  49.7 1.6 %copy.14 = f32[1,48,1024]{2,1,0:T(8,128)} copy(f32[1,48,1024]{2,1,0:T(8,128)} %bitcast.3) | data formatting | bytes 393216

commit v3 on v2

--- a/solution.py
+++ b/solution.py
@@ -10,7 +10,6 @@
 F32, BF16 = jnp.float32, jnp.bfloat16
 N = 4
 CH = 4
-WINDOW = 4
 MESH = pl.DeviceIdType.MESH
 
 
@@ -21,7 +20,7 @@
 def layer_kernel(
     tok, gates, routes, cot, wu, wd,
     mixed, gtok, gdown,
-    X, G, SC, Y, R, WU, WD, WG, pre, dh, hid, dpre, GD, S1, R1, S2, R2,
+    X, G, SC, Y, R, WU, WD, WG, pre, hid, GD, S1, R1, S2, R2,
     loc, ag_s, ag_r, rs_s, rs_r, g_s, g_r, p1_s, p1_r, p2_s, p2_r,
 ):
     T = tok.shape[0]
@@ -124,37 +123,20 @@
         ).wait_recv()
         return R[ph, c, rows(slot), :].astype(F32)
 
-    def rs_open(ph):
-        def fn(k, targets):
-            sent = [rs(ph, c, s, k) for s in targets for c in range(CH)]
-            for i, cp in enumerate(sent):
-                if i >= WINDOW:
-                    sent[i - WINDOW].wait_send()
-                cp.start()
-
-        pl.when(z == 0)(functools.partial(fn, 0, list(range(N - 1, 0, -1))))
-        pl.when(z == N - 1)(functools.partial(fn, N - 1, list(range(N - 1))))
-
-    def rs_left(k):
-        targets = list(range(N - 1, 0, -1)) if k == 0 else [s for s in range(N) if s != k]
-        every = [(s, c) for s in targets for c in range(CH)]
-        return every[-WINDOW:] if k in (0, N - 1) else every
+    def rs_open(ph, c, i):
+        pl.when(z == 0)(lambda: rs(ph, c, i, 0).start())
+        pl.when(z == N - 1)(lambda: rs(ph, c, N - 1 - i, N - 1).start())
 
     def rs_pass(ph):
-        def add(c, s, k, step):
-            got = rs_arrived(ph, c, s, k, step)
-            Y[ph, c, rows(s), :] = (Y[ph, c, rows(s), :].astype(F32) + got).astype(BF16)
-            rs(ph, c, s, k).start()
-
-        def fn(k, step, far, near, back_to):
-            for c in range(CH):
-                add(c, far, k, step)
-            for c in range(CH):
-                add(c, near, k, step)
-                add(c, back_to, k, -step)
-
-        pl.when(z == 1)(functools.partial(fn, 1, 1, 3, 2, 0))
-        pl.when(z == 2)(functools.partial(fn, 2, -1, 0, 1, 3))
+        def fn(k, order):
+            for s, step in order:
+                for c in range(CH):
+                    got = rs_arrived(ph, c, s, k, step)
+                    Y[ph, c, rows(s), :] = (Y[ph, c, rows(s), :].astype(F32) + got).astype(BF16)
+                    rs(ph, c, s, k).start()
+
+        pl.when(z == 1)(functools.partial(fn, 1, [(2, 1), (3, 1), (0, -1)]))
+        pl.when(z == 2)(functools.partial(fn, 2, [(1, -1), (0, -1), (3, 1)]))
 
     def rs_close(ph, c):
         out = (mixed, gtok)[ph]
@@ -185,45 +167,62 @@
 
     here(gate_open)
 
-    def up(c):
-        locals_["u", c].wait()
-        part = dot(X[c], WU[c], 1, 0)
-        pre[...] = part if c == 0 else pre[...] + part
-
-    for t in range(CH + 2):
-        if t < CH:
-            ag_step(0, t, 1)
-        if 0 <= t - 1 < CH:
-            ag_step(0, t - 1, 2)
-        if t == CH:
-            for c in range(CH):
-                locals_["g", c].wait()
-            ag_open(1)
-        if 0 <= t - 2 < CH:
-            ag_step(0, t - 2, 3)
-            up(t - 2)
-
     def gate_close(k):
         for s in range(N):
             if s != k:
                 gate(s, k).wait_recv()
 
-    here(gate_close)
-    wide = WG[...].astype(F32)
-    gcol = jnp.sum(
-        jnp.where(lax.broadcasted_iota(jnp.int32, wide.shape, 1) == z, wide, 0.0), axis=1, keepdims=True
-    )
-    v = pre[...]
-    hid[...] = (v / (1.0 + jnp.exp(-v))).astype(BF16)
-
-    def down(c):
-        locals_["d", c].wait()
-        Y[0, c] = (gcol * dot(hid[...], WD[c], 1, 0)).astype(BF16)
-
-    def back(c):
-        SC[c] = (gcol * G[c].astype(F32)).astype(BF16)
-        part = dot(SC[c], WD[c], 1, 1)
-        dh[...] = part if c == 0 else dh[...] + part
+    low = z < N // 2
+    inner = (z == 1) | (z == 2)
+    toward = jnp.where(low, 1, -1)
+    order = [
+        z,
+        jnp.where(inner, z - toward, z + toward),
+        jnp.where(inner, z + toward, z + 2 * toward),
+        jnp.where(inner, z + 2 * toward, z + 3 * toward),
+    ]
+    spans = [pl.ds(pl.multiple_of(s * T, T), T) for s in order]
+
+    def gate_column(at):
+        wide = WG[at, :].astype(F32)
+        mine = lax.broadcasted_iota(jnp.int32, wide.shape, 1) == z
+        return jnp.sum(jnp.where(mine, wide, 0.0), axis=1, keepdims=True)
+
+    def forward(i):
+        at = spans[i]
+        v = None
+        for c in range(CH):
+            if i == 0:
+                locals_["u", c].wait()
+            part = dot(X[c, at, :], WU[c], 1, 0)
+            v = part if c == 0 else v + part
+        pre[at, :] = v
+        h = (v / (1.0 + jnp.exp(-v))).astype(BF16)
+        hid[at, :] = h
+        gcol = gate_column(at)
+        for c in range(CH):
+            if i == 0:
+                locals_["d", c].wait()
+            Y[0, c, at, :] = (gcol * dot(h, WD[c], 1, 0)).astype(BF16)
+            if i:
+                rs_open(0, c, i)
+
+    def backward(i):
+        at = spans[i]
+        gcol = gate_column(at)
+        d = None
+        for c in range(CH):
+            scaled = (gcol * G[c, at, :].astype(F32)).astype(BF16)
+            SC[c, at, :] = scaled
+            part = dot(scaled, WD[c], 1, 1)
+            d = part if c == 0 else d + part
+        v = pre[at, :]
+        sig = 1.0 / (1.0 + jnp.exp(-v))
+        dp = (d * sig * (1.0 + v * (1.0 - sig))).astype(BF16)
+        for c in range(CH):
+            Y[1, c, at, :] = dot(dp, WU[c], 1, 1).astype(BF16)
+            if i:
+                rs_open(1, c, i)
 
     def plane1(m):
         return pltpu.make_async_remote_copy(
@@ -248,30 +247,37 @@
             S1[m] = GD[shard(2 * m + 1 - core), :].astype(BF16)
             plane1(m).start()
 
-    for c in range(CH):
-        down(c)
-    rs_open(0)
+    forward(0)
+    here(gate_close)
+    for c in range(CH):
+        ag_step(0, c, 1)
+    forward(1)
+    for c in range(CH):
+        ag_step(0, c, 2)
+    for c in range(CH):
+        locals_["g", c].wait()
+    ag_open(1)
+    forward(2)
+    for c in range(CH):
+        ag_step(0, c, 3)
+    forward(3)
+    backward(0)
     for c in range(CH):
         ag_step(1, c, 1)
+    backward(1)
     for c in range(CH):
         ag_step(1, c, 2)
+    backward(2)
     for c in range(CH):
         ag_step(1, c, 3)
-        back(c)
-        if c == CH // 2 - 1:
-            grads()
-
-    sig = 1.0 / (1.0 + jnp.exp(-pre[...]))
-    dpre[...] = (dh[...] * sig * (1.0 + pre[...] * (1.0 - sig))).astype(BF16)
-    for c in range(CH):
-        Y[1, c] = dot(dpre[...], WU[c], 1, 1).astype(BF16)
+    backward(3)
+    grads()
+    rs_pass(0)
     for m in range(4):
         plane1(m).wait_recv()
     for d in range(1, 4):
         S2[d - 1] = (GD[shard(2 * mates[d] + core), :] + R1[mates[d]].astype(F32)).astype(BF16)
         plane2(d).start()
-    rs_open(1)
-    rs_pass(0)
     rs_pass(1)
     for c in range(CH):
         rs_close(0, c)
@@ -289,8 +295,9 @@
                 for h in range(N - 1):
                     for cp in ag_sends(ph, c, k, h):
                         cp.wait_send()
-            for s, c in rs_left(k):
-                rs(ph, c, s, k).wait_send()
+                for s in range(N):
+                    if s != k:
+                        rs(ph, c, s, k).wait_send()
         for s in range(N):
             if s != k:
                 gate(k, s).wait_send()
@@ -331,8 +338,6 @@
             pltpu.VMEM((CH, FF, W), BF16),
             pltpu.VMEM((A, 128), BF16),
             pltpu.VMEM((A, FF), F32),
-            pltpu.VMEM((A, FF), F32),
-            pltpu.VMEM((A, FF), BF16),
             pltpu.VMEM((A, FF), BF16),
             pltpu.VMEM((hw, dw), F32),
             pltpu.VMEM((4, sh, dw), BF16),

time: 51.5 us -> 55 us (1.068)
  Pallas kernels: 45.9 us -> 49.5 us
    pallas_call x1, Pallas kernels: 45.9 us -> 49.5 us  [fused(): pl.pallas_call(layer_kernel, out_shape=(jax.ShapeDtypeStruct((T, D), BF16...]
where the time goes in v3:
time: 55 us; the launch traced here: 54.8 us
  Pallas kernels  49.5 us (90%)
  local copies, waits for them, and re-layouts  4.75 us (9%)
  between operations  0.64 us (1%)
    pallas_call x1, Pallas kernels, fused(): pl.pallas_call(layer_kernel, out_shape=(jax.ShapeDtypeStruct((T, D), BF16...  49.5 us
    unnamed x3, local copies, waits for them, and re-layouts  4.75 us

profile of v3, /device:TPU:0, one launch (start us, length us, event | category | flops | bytes accessed | tf_op | source)
XLA Modules:
  0.0 54.8 jit_solution(15131548946453504392)
XLA Ops:
  0.6 49.5 %shard_map.85 = (bf16[32,2048]{1,0:T(8,128)(2,1)}, bf16[32,2048]{1,0:T(8,128)(2,1)}, f32[48,1024]{1,0:T(8,128)}) custom-call(bf16[32,2048]{1,0:T(8,128)(2,1)} %tok.1, bf16[2,32]{1,0:T(2,128)(2,1)} %bitcast.5, s32[2,32]{1,0:T(2,128)} %bitcast.4, bf16[32,2048]{1,0:T(8,128)(2,1)} %cot.1, bf16[1,2048,768]{2,1,0:T(8,128)(2,1)} %wu.1, bf16[1,768,2048]{2,1,0:T(8,128)(2,1)} %wd.1), custom_call_target="tpu_custom_call" | custom-call | tf_op jit(solution)/shard_map/pallas_call | solution.py:322
  50.1 1.6 %copy.12 = bf16[32,2048]{1,0:T(8,128)(2,1)} copy(bf16[32,2048]{1,0:T(8,128)(2,1)} %get-tuple-element.12) | data formatting | bytes 262144
  51.7 1.6 %copy.13 = bf16[32,2048]{1,0:T(8,128)(2,1)} copy(bf16[32,2048]{1,0:T(8,128)(2,1)} %get-tuple-element.13) | data formatting | bytes 262144
  53.2 1.6 %copy.14 = f32[1,48,1024]{2,1,0:T(8,128)} copy(f32[1,48,1024]{2,1,0:T(8,128)} %bitcast.3) | data formatting | bytes 393216

commit v4 on v2

--- a/solution.py
+++ b/solution.py
@@ -124,13 +124,13 @@
         ).wait_recv()
         return R[ph, c, rows(slot), :].astype(F32)
 
-    def rs_open(ph):
+    def rs_open(ph, first, last):
         def fn(k, targets):
             sent = [rs(ph, c, s, k) for s in targets for c in range(CH)]
-            for i, cp in enumerate(sent):
+            for i in range(first, last):
                 if i >= WINDOW:
                     sent[i - WINDOW].wait_send()
-                cp.start()
+                sent[i].start()
 
         pl.when(z == 0)(functools.partial(fn, 0, list(range(N - 1, 0, -1))))
         pl.when(z == N - 1)(functools.partial(fn, N - 1, list(range(N - 1))))
@@ -250,27 +250,30 @@
 
     for c in range(CH):
         down(c)
-    rs_open(0)
+        rs_open(0, c, c + 1)
     for c in range(CH):
         ag_step(1, c, 1)
+    rs_open(0, CH, 2 * CH)
     for c in range(CH):
         ag_step(1, c, 2)
     for c in range(CH):
         ag_step(1, c, 3)
         back(c)
-        if c == CH // 2 - 1:
-            grads()
+        rs_open(0, 2 * CH + c, 2 * CH + c + 1)
 
     sig = 1.0 / (1.0 + jnp.exp(-pre[...]))
     dpre[...] = (dh[...] * sig * (1.0 + pre[...] * (1.0 - sig))).astype(BF16)
     for c in range(CH):
         Y[1, c] = dot(dpre[...], WU[c], 1, 1).astype(BF16)
+        rs_open(1, c, c + 1)
+    grads()
+    rs_open(1, CH, 2 * CH)
     for m in range(4):
         plane1(m).wait_recv()
     for d in range(1, 4):
         S2[d - 1] = (GD[shard(2 * mates[d] + core), :] + R1[mates[d]].astype(F32)).astype(BF16)
         plane2(d).start()
-    rs_open(1)
+    rs_open(1, 2 * CH, 3 * CH)
     rs_pass(0)
     rs_pass(1)
     for c in range(CH):

time: 51.5 us -> 52.1 us (1.012)
  no operation moved by 1% of the time
where the time goes in v4:
time: 52.1 us; the launch traced here: 51.5 us
  Pallas kernels  46.1 us (88%)
  local copies, waits for them, and re-layouts  4.75 us (9%)
  between operations  0.64 us (1%)
    pallas_call x1, Pallas kernels, fused(): pl.pallas_call(layer_kernel, out_shape=(jax.ShapeDtypeStruct((T, D), BF16...  46.1 us
    unnamed x3, local copies, waits for them, and re-layouts  4.75 us

profile of v4, /device:TPU:0, one launch (start us, length us, event | category | flops | bytes accessed | tf_op | source)
XLA Modules:
  0.0 51.5 jit_solution(8798240304306739497)
XLA Ops:
  0.6 46.1 %shard_map.85 = (bf16[32,2048]{1,0:T(8,128)(2,1)}, bf16[32,2048]{1,0:T(8,128)(2,1)}, f32[48,1024]{1,0:T(8,128)}) custom-call(bf16[32,2048]{1,0:T(8,128)(2,1)} %tok.1, bf16[2,32]{1,0:T(2,128)(2,1)} %bitcast.5, s32[2,32]{1,0:T(2,128)} %bitcast.4, bf16[32,2048]{1,0:T(8,128)(2,1)} %cot.1, bf16[1,2048,768]{2,1,0:T(8,128)(2,1)} %wu.1, bf16[1,768,2048]{2,1,0:T(8,128)(2,1)} %wd.1), custom_call_target="tpu_custom_call" | custom-call | tf_op jit(solution)/shard_map/pallas_call | solution.py:318
  46.7 1.6 %copy.12 = bf16[32,2048]{1,0:T(8,128)(2,1)} copy(bf16[32,2048]{1,0:T(8,128)(2,1)} %get-tuple-element.12) | data formatting | bytes 262144
  48.3 1.6 %copy.13 = bf16[32,2048]{1,0:T(8,128)(2,1)} copy(bf16[32,2048]{1,0:T(8,128)(2,1)} %get-tuple-element.13) | data formatting | bytes 262144
  49.8 1.6 %copy.14 = f32[1,48,1024]{2,1,0:T(8,128)} copy(f32[1,48,1024]{2,1,0:T(8,128)} %bitcast.3) | data formatting | bytes 393216

commit v5 on v4

--- a/solution.py
+++ b/solution.py
@@ -250,30 +250,28 @@
 
     for c in range(CH):
         down(c)
-        rs_open(0, c, c + 1)
+    rs_open(0, 0, 3 * CH)
     for c in range(CH):
         ag_step(1, c, 1)
-    rs_open(0, CH, 2 * CH)
     for c in range(CH):
         ag_step(1, c, 2)
     for c in range(CH):
         ag_step(1, c, 3)
         back(c)
-        rs_open(0, 2 * CH + c, 2 * CH + c + 1)
+        if c == CH // 2 - 1:
+            grads()
 
     sig = 1.0 / (1.0 + jnp.exp(-pre[...]))
     dpre[...] = (dh[...] * sig * (1.0 + pre[...] * (1.0 - sig))).astype(BF16)
     for c in range(CH):
         Y[1, c] = dot(dpre[...], WU[c], 1, 1).astype(BF16)
         rs_open(1, c, c + 1)
-    grads()
-    rs_open(1, CH, 2 * CH)
     for m in range(4):
         plane1(m).wait_recv()
     for d in range(1, 4):
         S2[d - 1] = (GD[shard(2 * mates[d] + core), :] + R1[mates[d]].astype(F32)).astype(BF16)
         plane2(d).start()
-    rs_open(1, 2 * CH, 3 * CH)
+    rs_open(1, CH, 3 * CH)
     rs_pass(0)
     rs_pass(1)
     for c in range(CH):
@@ -303,6 +301,17 @@
         plane1(m).wait_send()
     for d in range(1, 4):
         plane2(d).wait_send()
+
+
+def hand_over(a, b, c, a_out, b_out, c_out, sem):
+    copies = [
+        pltpu.make_async_copy(src, dst, sem.at[i])
+        for i, (src, dst) in enumerate(((a, a_out), (b, b_out), (c, c_out)))
+    ]
+    for cp in copies:
+        cp.start()
+    for cp in copies:
+        cp.wait()
 
 
 def fused(tokens, gates, routes, cotangent, up_weight, down_weight):
@@ -358,6 +367,14 @@
             collective_id=0, has_side_effects=True, vmem_limit_bytes=60 * 1024 * 1024
         ),
     )(tokens, gates.T, routes.T, cotangent, up_weight, down_weight)
+    results = (mixed, gtok, gdown)
+    mixed, gtok, gdown = pl.pallas_call(
+        hand_over,
+        out_shape=tuple(jax.ShapeDtypeStruct(r.shape, r.dtype) for r in results),
+        in_specs=[anyspace] * 3,
+        out_specs=(anyspace,) * 3,
+        scratch_shapes=[dma((3,))],
+    )(*results)
     return (mixed, gtok, gdown[None])
 
 

time: 52.1 us -> 62.4 us (1.20)
  Pallas kernels: 46.1 us -> 61.5 us
  local copies, waits for them, and re-layouts: 4.75 us -> 0 us
    pallas_call x0 -> x1, Pallas kernels: none -> 15 us  [fused(): pl.pallas_call(hand_over, out_shape=tuple((jax.ShapeDtypeStruct(r.shape,...]
    unnamed x3 -> x0, local copies, waits for them, and re-layouts: 4.75 us -> none
where the time goes in v5:
time: 62.4 us; the launch traced here: 62.2 us
  Pallas kernels  61.5 us (99%)
  between operations  0.64 us (1%)
    pallas_call x1, Pallas kernels, fused(): pl.pallas_call(layer_kernel, out_shape=(jax.ShapeDtypeStruct((T, D), BF16...  46.5 us
    pallas_call x1, Pallas kernels, fused(): pl.pallas_call(hand_over, out_shape=tuple((jax.ShapeDtypeStruct(r.shape,...  15 us

profile of v5, /device:TPU:0, one launch (start us, length us, event | category | flops | bytes accessed | tf_op | source)
XLA Modules:
  0.0 62.2 jit_solution(4487108365837244549)
XLA Ops:
  0.6 46.5 %shard_map.85 = (bf16[32,2048]{1,0:T(8,128)(2,1)}, bf16[32,2048]{1,0:T(8,128)(2,1)}, f32[48,1024]{1,0:T(8,128)}) custom-call(bf16[32,2048]{1,0:T(8,128)(2,1)} %tok.1, bf16[2,32]{1,0:T(2,128)(2,1)} %bitcast.4, s32[2,32]{1,0:T(2,128)} %bitcast.3, bf16[32,2048]{1,0:T(8,128)(2,1)} %cot.1, bf16[1,2048,768]{2,1,0:T(8,128)(2,1)} %wu.1, bf16[1,768,2048]{2,1,0:T(8,128)(2,1)} %wd.1), custom_call_target="tpu_custom_call" | custom-call | tf_op jit(solution)/shard_map/pallas_call | solution.py:327
  47.2 15.0 %shard_map.86 = (bf16[32,2048]{1,0:T(8,128)(2,1)}, bf16[32,2048]{1,0:T(8,128)(2,1)}, f32[48,1024]{1,0:T(8,128)}) custom-call(bf16[32,2048]{1,0:T(8,128)(2,1)} %get-tuple-element.9.a, bf16[32,2048]{1,0:T(8,128)(2,1)} %get-tuple-element.10.b, f32[48,1024]{1,0:T(8,128)} %get-tuple-element.11.c), custom_call_target="tpu_custom_call" | custom-call | tf_op jit(solution)/shard_map/pallas_call | solution.py:371
